TPU v7x, 256 devices: a whole 4x4x8 slice. The times are simulated.
256 devices in a mesh: req: 8 (over y, core), mp: 32 (over z, x).
Axes of the slice: x: 4, y: 4, z: 8, core: 2. Of those that a mesh axis runs over, the one named last changes fastest.
Arguments:
- draft_hidden: bfloat16 [16, 2048], P('req'), may hold values from -6 to 6
- draft_weight: bfloat16 [4, 2048, 2048], P(None, None, 'mp'), may hold values from -0.125 to 0.125
- vocab_weight: bfloat16 [98304, 2048], P(('req', 'mp')), may hold values from -0.375 to 0.375
- tree_inputs: bfloat16 [768, 2048], P('req')
- tree_parent: int32 [16, 48], P('req'), may hold values from -1 to 41, as said below
- cache_len: int32 [16], P('req'), may hold values from 1 to 8192, as said below
- page_table: int32 [16, 64], P('req'), may hold values from -1 to 1023, as said below
- kv_cache: bfloat16 [1024, 2, 128, 2048], P(('req', 'mp'))
- accepted_node: int32 [16], P('req'), may hold values from 0 to 47
- qkv_weight: bfloat16 [2048, 3, 2048], P(None, None, 'mp'), may hold values from -0.125 to 0.125
- norm_gains: bfloat16 [4, 2048], replicated, may hold values from 0.5 to 1.5
- out_weight: bfloat16 [2048, 2048], P(None, 'mp'), may hold values from -0.125 to 0.125
- gate_up_weight: bfloat16 [2048, 2, 8192], P(None, None, 'mp'), may hold values from -0.125 to 0.125
- down_weight: bfloat16 [8192, 2048], P('mp'), may hold values from -0.0625 to 0.0625
Outputs:
- draft_logits: float32 [16, 4, 98304], P(None, None, ('req', 'mp'))
- layer_out: bfloat16 [768, 2048], P(('req', 'mp'))
- accepted_kv: bfloat16 [16, 4, 2, 2048], P('req', None, None, 'mp')
Inputs may be any that keep to these rules, and one draw needn't show every extreme that they name: `page_table`: row r lists the pool pages of request r in the order of its tokens, ceil(cache_len[r] / 128) of them, then -1. The pages of the requests of one index of req lie in that index's part of kv_cache, and no page serves two requests. `cache_len`: on every index of req some request has exactly 8192 cached tokens. `tree_parent`: A parent has a smaller index than its child; a node has at most 3 ancestors.
All inputs are finite; a program needn't handle non-finite values.
Results may differ from a plain program's by a relative error of at most 0.01355.
Values may be sent and summed in bfloat16 or wider, within the bound.
No kernel may reach another device: no remote copies, remote signals or barrier semaphores. Data moves between devices by JAX's collectives and lax.ppermute only.
A program may use at most 128 MiB of HBM per device.

v0:
```python
import jax
import jax.numpy as jnp
from jax import lax
from jax.sharding import PartitionSpec as P

HEADS = 16
HEAD_DIM = 128
rope_base = 500000.0
norm_epsilon = 1e-06
masked_score = -1e30


def combined_all(part, axis, combine):
    gathered = jax.tree.map(lambda a: lax.all_gather(a, axis), part)

    def take(source):
        return jax.tree.map(lambda a: lax.dynamic_index_in_dim(a, source, 0, False), gathered)

    return lax.fori_loop(
        1, lax.axis_size(axis), lambda source, state: combine(state, take(source)), take(0)
    )


def rms_scaled(entries, gain_row):
    mean_square = jnp.mean(entries * entries, axis=-1, keepdims=True)
    return entries * lax.rsqrt(mean_square + norm_epsilon) * gain_row


def tree_shape(parents):
    node_count = parents.shape[-1]
    step_one = (
        parents[..., :, None] == jnp.arange(node_count, dtype=jnp.int32)[None, None, :]
    ).astype(jnp.float32)
    step_two = jnp.einsum("rij,rjk->rik", step_one, step_one, precision=lax.Precision.HIGHEST)
    step_three = jnp.einsum("rij,rjk->rik", step_two, step_one, precision=lax.Precision.HIGHEST)
    ancestry = jnp.eye(node_count, dtype=jnp.float32)[None] + step_one + step_two + step_three
    return (ancestry, jnp.sum(ancestry, axis=-1))


def rotate(entries, positions):
    row_count = entries.shape[0]
    half_dim = HEAD_DIM // 2
    shaped = entries.reshape(row_count, HEADS, HEAD_DIM)
    freqs = rope_base ** (-jnp.arange(half_dim, dtype=jnp.float32) * 2.0 / HEAD_DIM)
    angles = positions[:, None] * freqs[None, :]
    cosine = jnp.cos(angles)[:, None, :]
    sine_part = jnp.sin(angles)[:, None, :]
    front = shaped[..., :half_dim]
    back_half = shaped[..., half_dim:]
    turned = jnp.concatenate(
        [front * cosine - back_half * sine_part, back_half * cosine + front * sine_part], axis=-1
    )
    return turned.reshape(row_count, HEADS * HEAD_DIM)


def fold_states(left_state, right_state):
    top_left, total_left, mixed_left = left_state
    top_right, total_right, mixed_right = right_state
    top_both = jnp.maximum(top_left, top_right)
    factor_left = jnp.exp(top_left - top_both)
    factor_right = jnp.exp(top_right - top_both)
    return (
        top_both,
        total_left * factor_left + total_right * factor_right,
        mixed_left * factor_left[..., None] + mixed_right * factor_right[..., None],
    )


def tree_states(query_part, key_part, value_part, ancestry):
    scale = HEAD_DIM ** (-0.5)
    scores = (
        jnp.einsum("rthe,rshe->rths", query_part, key_part, preferred_element_type=jnp.float32)
        * scale
    )
    visible = (ancestry > 0.5)[:, :, None, :]
    scores = jnp.where(visible, scores, masked_score)
    top_score = jnp.max(scores, axis=-1)
    weights = jnp.where(visible, jnp.exp(scores - top_score[..., None]), 0.0)
    totals = jnp.sum(weights, axis=-1)
    mixed = jnp.einsum(
        "rths,rshe->rthe",
        weights.astype(jnp.bfloat16),
        value_part,
        preferred_element_type=jnp.float32,
    )
    return (top_score, totals, mixed)


def page_states(queries, cache_len, page_table, kv_cache, first_slot):
    scale = HEAD_DIM ** (-0.5)
    page_count = kv_cache.shape[0]
    page_len = kv_cache.shape[2]
    table_width = page_table.shape[1]
    req_local = page_table.shape[0]
    slots = first_slot + jnp.arange(page_count, dtype=jnp.int32)
    matches = page_table[None, :, :] == slots[:, None, None]
    owner_hot = jnp.any(matches, axis=2)
    page_index = jnp.sum(
        jnp.where(matches, jnp.arange(table_width, dtype=jnp.int32)[None, None, :], 0), axis=(1, 2)
    )
    owner = jnp.sum(
        jnp.where(matches, jnp.arange(req_local, dtype=jnp.int32)[None, :, None], 0), axis=(1, 2)
    )
    in_use = jnp.any(matches, axis=(1, 2))
    limit = jnp.take(cache_len, owner)
    token_pos = page_index[:, None] * page_len + jnp.arange(page_len, dtype=jnp.int32)[None, :]
    valid = in_use[:, None] & (token_pos < limit[:, None])
    page_keys = kv_cache[:, 0].reshape(page_count, page_len, HEADS, HEAD_DIM)
    page_values = kv_cache[:, 1].reshape(page_count, page_len, HEADS, HEAD_DIM)
    asked = jnp.take(queries, owner, axis=0)
    scores = (
        jnp.einsum("pthe,pshe->phts", asked, page_keys, preferred_element_type=jnp.float32) * scale
    )
    visible = valid[:, None, None, :]
    scores = jnp.where(visible, scores, masked_score)
    top_score = jnp.max(scores, axis=-1)
    weights = jnp.where(visible, jnp.exp(scores - top_score[..., None]), 0.0)
    totals = jnp.sum(weights, axis=-1)
    mixed = jnp.einsum(
        "phts,pshe->pthe",
        weights.astype(jnp.bfloat16),
        page_values,
        preferred_element_type=jnp.float32,
    )
    owner_mask = owner_hot[:, :, None, None]
    top_request = jnp.max(jnp.where(owner_mask, top_score[:, None], masked_score), axis=0)
    spread_gap = jnp.where(owner_mask, top_score[:, None] - top_request[None], 0.0)
    factor = jnp.where(owner_mask, jnp.exp(spread_gap), 0.0)
    total_request = jnp.sum(factor * totals[:, None], axis=0)
    mixed_request = jnp.einsum("prht,pthe->rthe", factor, mixed, precision=lax.Precision.HIGHEST)
    return (
        jnp.transpose(top_request, (0, 2, 1)),
        jnp.transpose(total_request, (0, 2, 1)),
        mixed_request,
    )


def per_device(
    draft_hidden,
    draft_weight,
    vocab_weight,
    tree_inputs,
    tree_parent,
    cache_len,
    page_table,
    kv_cache,
    accepted_node,
    qkv_weight,
    norm_gains,
    out_weight,
    gate_up_weight,
    down_weight,
):
    mp_count = lax.axis_size("mp")
    req_count = lax.axis_size("req")
    mp_place = lax.axis_index("mp")
    req_place = lax.axis_index("req")
    req_local = draft_hidden.shape[0]
    model_width = draft_hidden.shape[1]
    draft_count = draft_weight.shape[0]
    slab_width = draft_weight.shape[2]
    vocab_local = vocab_weight.shape[0]
    draft_raw = jnp.einsum(
        "rd,kde->rke", draft_hidden, draft_weight, preferred_element_type=jnp.float32
    )
    own_columns = lax.dynamic_slice_in_dim(
        draft_hidden, mp_place * slab_width, slab_width, 1
    ).astype(jnp.float32)
    drafted = (own_columns[:, None, :] + jax.nn.silu(draft_raw)).astype(jnp.bfloat16)
    collected = lax.all_gather(drafted[None], ("req", "mp"), axis=0, tiled=True)
    collected = collected.reshape(req_count, mp_count, req_local, draft_count, slab_width)
    vocab_table = vocab_weight.reshape(vocab_local, mp_count, slab_width)
    draft_logits = jnp.einsum(
        "gmrkc,vmc->grkv", collected, vocab_table, preferred_element_type=jnp.float32
    ).reshape(req_count * req_local, draft_count, vocab_local)
    row_count = tree_inputs.shape[0]
    tree_size = tree_parent.shape[1]
    own_projection = jnp.einsum(
        "td,dce->tce", tree_inputs, qkv_weight, preferred_element_type=jnp.float32
    ).astype(jnp.bfloat16)
    projected = lax.all_gather(own_projection, "mp", axis=2, tiled=True)
    ancestry, node_depth = tree_shape(tree_parent)
    positions = (cache_len[:, None].astype(jnp.float32) + node_depth - 1.0).reshape(row_count)
    gain_rows = norm_gains.astype(jnp.float32)
    queries = (
        rotate(rms_scaled(projected[:, 0].astype(jnp.float32), gain_rows[0]), positions)
        .astype(jnp.bfloat16)
        .reshape(req_local, tree_size, HEADS, HEAD_DIM)
    )
    keys_tree = (
        rotate(rms_scaled(projected[:, 1].astype(jnp.float32), gain_rows[1]), positions)
        .astype(jnp.bfloat16)
        .reshape(req_local, tree_size, HEADS, HEAD_DIM)
    )
    values_tree = projected[:, 2].reshape(req_local, tree_size, HEADS, HEAD_DIM)
    chosen = (accepted_node[:, None] == jnp.arange(tree_size, dtype=jnp.int32)[None, :]).astype(
        jnp.float32
    )
    on_path = jnp.einsum("rt,rts->rs", chosen, ancestry, precision=lax.Precision.HIGHEST)
    levels = jnp.arange(1, draft_count + 1, dtype=jnp.float32)
    picker = on_path[:, None, :] * (node_depth[:, None, :] == levels[None, :, None]).astype(
        jnp.float32
    )
    key_columns = lax.dynamic_slice_in_dim(
        keys_tree.reshape(req_local, tree_size, model_width), mp_place * slab_width, slab_width, 2
    )
    value_columns = own_projection[:, 2].reshape(req_local, tree_size, slab_width)
    stacked = jnp.stack([key_columns, value_columns], axis=2)
    accepted_kv = jnp.einsum(
        "rjs,rsce->rjce", picker.astype(jnp.bfloat16), stacked, preferred_element_type=jnp.float32
    ).astype(jnp.bfloat16)
    first_slot = (req_place * mp_count + mp_place) * kv_cache.shape[0]
    page_part = page_states(queries, cache_len, page_table, kv_cache, first_slot)
    identity = (
        jnp.full((req_local, tree_size, HEADS), masked_score, jnp.float32),
        jnp.zeros((req_local, tree_size, HEADS), jnp.float32),
        jnp.zeros((req_local, tree_size, HEADS, HEAD_DIM), jnp.float32),
    )
    tree_part = lax.cond(
        mp_place == 0,
        lambda: tree_states(queries, keys_tree, values_tree, ancestry),
        lambda: identity,
    )
    local_state = fold_states(page_part, tree_part)
    merged = combined_all(local_state, "mp", fold_states)
    attended = (
        (merged[2] / merged[1][..., None]).astype(jnp.bfloat16).reshape(row_count, model_width)
    )
    out_columns = jnp.dot(attended, out_weight, preferred_element_type=jnp.float32).astype(
        jnp.bfloat16
    )
    projected_out = lax.all_gather(out_columns, "mp", axis=1, tiled=True)
    residual = (
        tree_inputs.astype(jnp.float32)
        + rms_scaled(projected_out.astype(jnp.float32), gain_rows[2])
    ).astype(jnp.bfloat16)
    gate_up = jnp.einsum(
        "td,dce->tce", residual, gate_up_weight, preferred_element_type=jnp.float32
    )
    hidden = (jax.nn.silu(gate_up[:, 0]) * gate_up[:, 1]).astype(jnp.bfloat16)
    row_share = row_count // mp_count
    first_row = mp_place * row_share
    summed = lax.psum(
        jnp.dot(hidden, down_weight, preferred_element_type=jnp.float32).astype(jnp.bfloat16), "mp"
    ).astype(jnp.float32)
    own_rows = lax.dynamic_slice_in_dim(summed, first_row, row_share, 0)
    residual_rows = lax.dynamic_slice_in_dim(residual, first_row, row_share, 0).astype(jnp.float32)
    layer_out = (residual_rows + rms_scaled(own_rows, gain_rows[3])).astype(jnp.bfloat16)
    return (draft_logits, layer_out, accepted_kv)


def solution(mesh):
    placed = (
        P("req", None),
        P(None, None, "mp"),
        P(("req", "mp"), None),
        P("req", None),
        P("req", None),
        P("req"),
        P("req", None),
        P(("req", "mp"), None, None, None),
        P("req"),
        P(None, None, "mp"),
        P(),
        P(None, "mp"),
        P(None, None, "mp"),
        P("mp", None),
    )
    return jax.shard_map(
        per_device,
        mesh=mesh,
        in_specs=placed,
        out_specs=(
            P(None, None, ("req", "mp")),
            P(("req", "mp"), None),
            P("req", None, None, "mp"),
        ),
        check_vma=False,
    )
```

profile of v0, /device:TPU:8, one launch (start us, length us, event | category | flops | bytes accessed | tf_op | source)
XLA Modules:
  0.0 613.0 jit_solution(11031418135957718343)
XLA Ops:
  7.2 1.7 fusion.81
  13.2 4.8 fusion.77
  18.1 4.0 copy.281
  22.0 4.0 copy.280
  27.2 64.1 %all-gather.7.cloned.1.call-done = bf16[96,3,2048]{0,2,1:T(8,128)(2,1)} async-done(((bf16[96,3,64]{0,2,1:T(8,128)(2,1)}), bf16[96,3,2048]{0,2,1:T(8,128)(2,1)}) %all-gather.7.cloned.1.call-update) | async-done | bytes 1179664 | tf_op jit(solution)/shard_map/all_gather | solution.py:181
  91.3 2.3 slice_convert_fusion.1
  93.6 2.5 copy.242
  96.1 1.3 copy.250
  97.4 1.6 multiply_reduce_fusion.1
  99.0 1.3 multiply_multiply_fusion.1
  100.5 1.3 multiply_subtract_fusion
  103.2 3.5 fusion.80
  107.0 2.4 fusion.20
  109.4 4.4 convolution_bitcast_fusion.1
  115.9 8.8 %fusion.17 = f32[48,16,128,2]{2,3,1,0:T(2,128)} fusion(f32[4,48,16,128]{3,1,2,0:T(8,128)} %convolution_bitcast_fusion.1, pred[4,2]{0,1:T(4,128)(4,1)S(1)} %get-tuple-element.271, f32[2,16,48]{0,1,2:T(8,128)S(1)} %select_reduce_fusion, f32[4,16,48]{0,1,2:T(8,128)S(1)} %copy.248), kind=kOutput, calls=%fused_computation.29 | convolution fusion | flops 9455616 | bytes 2377736 | tf_op jit(solution)/shard_map/prht,pthe->rthe/dot_general | solution.py:130
  124.7 2.8 multiply_reduce_fusion.2
  128.7 2.1 pad_maximum_fusion
  130.8 7.8 %conditional.1 = (f32[2,48,16]{1,2,0:T(8,128)}, f32[2,48,16]{1,2,0:T(8,128)S(1)}, f32[2,48,16,128]{3,2,1,0:T(8,128)S(1)}) conditional(s32[]{:T(128)} %convert_element_type.124, () %tuple.38, (f32[2,48,48]{1,2,0:T(8,128)S(1)}, bf16[96,16,128]{2,1,0:T(8,128)(2,1)}, bf16[2,48,16,128]{3,2,1,0:T(8,128)(2,1)S(1)}, bf16[96,3,2048]{0,2,1:T(8,128)(2,1)}) %tuple.104), branch_computations={%region_9.10_spmd, %region_10.13_spmd} | conditional | flops 38413824 | bytes 8417304 | solution.py:219
  130.8 2.5 copy.252
  134.4 2.0 fusion.76
  138.6 1.3 fusion.52
  140.1 2.5 fusion.26
  144.2 1.7 fusion.54
  146.0 69.4 %all-gather = bf16[512,4,64]{2,1,0:T(4,128)(2,1)S(1)} all-gather(bf16[2,4,64]{2,1,0:T(4,128)(2,1)S(1)} %add_convert_fusion.1), channel_id=2, replica_groups=mesh['req'=8,'mp'=32] {'req','mp'}, dimensions={0}, use_global_device_ids=true | all-gather | bytes 263168 | tf_op jit(solution)/shard_map/all_gather | solution.py:170
  215.8 2.7 copy.241
  218.5 1.8 convolution_bitcast_fusion.2
  221.9 46.9 %all-gather.2 = f32[64,48,16]{1,2,0:T(8,128)S(1)} all-gather(f32[2,48,16]{1,2,0:T(8,128)S(1)} %copy-done.9), channel_id=4, replica_groups=mesh['req'=8,'mp'=32] {'mp'}, dimensions={0}, use_global_device_ids=true | all-gather | bytes 202752 | tf_op jit(solution)/shard_map/all_gather | solution.py:14
  268.7 50.1 %all-gather.1 = f32[64,48,16]{1,2,0:T(8,128)S(1)} all-gather(f32[2,48,16]{1,2,0:T(8,128)S(1)} %get-tuple-element.307), channel_id=3, replica_groups=mesh['req'=8,'mp'=32] {'mp'}, dimensions={0}, use_global_device_ids=true | all-gather | bytes 202752 | tf_op jit(solution)/shard_map/all_gather | solution.py:14
  319.7 6.9 %all-gather.9.cloned.1.call-done = f32[64,48,16,128]{3,2,1,0:T(8,128)} async-done(((f32[2,48,16,128]{3,2,1,0:T(8,128)}), f32[64,48,16,128]{3,2,1,0:T(8,128)}) %all-gather.9.cloned.1.call-update) | async-done | bytes 25165840 | tf_op jit(solution)/shard_map/all_gather | solution.py:14
  327.7 80.2 %while.19 = (s32[]{:T(128)}, f32[2,48,16]{1,2,0:T(8,128)S(1)}, f32[2,48,16]{1,2,0:T(8,128)S(1)}, f32[2,48,16,128]{3,2,1,0:T(8,128)S(1)}, f32[32,2,48,16]{2,3,1,0...) while((s32[]{:T(128)}, f32[2,48,16]{1,2,0:T(8,128)S(1)}, ...), condition=%wide.region_16.17_spmd, body=%wide.region_15.16_spmd.sunk | while | flops 599045 | bytes 2445455 | solution.py:19
  328.7 1.7 fusion.96
  331.2 1.7 fusion.96
  333.8 1.7 fusion.96
  336.4 1.7 fusion.96
  339.0 1.7 fusion.96
  341.6 1.7 fusion.96
  344.2 1.7 fusion.96
  346.8 1.7 fusion.96
  349.4 1.7 fusion.96
  352.0 1.7 fusion.96
  354.5 1.7 fusion.96
  357.1 1.7 fusion.96
  359.7 1.7 fusion.96
  362.3 1.7 fusion.96
  364.9 1.7 fusion.96
  367.5 1.7 fusion.96
  370.1 1.7 fusion.96
  372.7 1.7 fusion.96
  375.3 1.7 fusion.96
  377.8 1.7 fusion.96
  380.4 1.7 fusion.96
  383.0 1.7 fusion.96
  385.6 1.7 fusion.96
  388.2 1.7 fusion.96
  390.8 1.7 fusion.96
  393.4 1.7 fusion.96
  396.0 1.7 fusion.96
  398.5 1.7 fusion.96
  401.1 1.7 fusion.96
  403.7 1.7 fusion.96
  406.3 1.7 fusion.96
  409.6 47.5 %all_gather.35 = bf16[96,2048]{0,1:T(8,128)(2,1)S(1)} all-gather(bf16[96,64]{0,1:T(8,128)(2,1)S(1)} %convolution_convert_fusion.1), channel_id=1, replica_groups=mesh['req'=8,'mp'=32] {'mp'}, dimensions={1}, use_global_device_ids=true | all-gather | bytes 405504 | tf_op jit(solution)/shard_map/all_gather | solution.py:232
  462.2 141.7 %all-reduce.2.cloned.1.call-done = bf16[96,2048]{1,0:T(8,128)(2,1)} async-done(((bf16[96,2048]{1,0:T(8,128)(2,1)}), bf16[96,2048]{1,0:T(8,128)(2,1)}) %all-reduce.2.cloned.1.call-update) | async-done | bytes 393232 | tf_op jit(solution)/shard_map/psum | solution.py:243
  604.9 1.5 fusion.47
  (203 shorter events, 55.0 us)
Async XLA Ops:
  7.2 450.6 %copy-start = (bf16[2048,2,256]{2,1,0:T(2,128)(2,1)S(1)}, bf16[2048,2,256]{2,1,0:T(2,128)(2,1)}, u32[]{:S(2)}) copy-start(bf16[2048,2,256]{2,1,0:T(2,128)(2,1)} %param.30) | copy-start | bytes 6291460
  7.2 5.2 copy-start.1
  7.2 5.0 copy-start.14
  7.2 84.1 %all-gather.7.cloned.1.call-start = ((), (), s32[]{:S(2)}) async-start(), calls=%async_computation | async-start | bytes 1622016 | tf_op jit(solution)/shard_map/all_gather | solution.py:181
  9.7 316.9 %all-gather.9.cloned.1.call-start = ((), (), s32[]{:S(2)}) async-start(), calls=%async_computation.2 | async-start | bytes 25952256 | tf_op jit(solution)/shard_map/all_gather | solution.py:14
  12.4 5.7 copy-start.15
  22.0 4.0 copy-start.17
  22.0 4.6 copy-start.8
  97.4 2.9 copy-start.3
  107.0 2.4 copy-start.2
  115.9 8.8 %copy-start.5 = (f32[4,16,48]{0,1,2:T(8,128)S(1)}, f32[4,16,48]{0,1,2:T(8,128)}, u32[]{:S(2)}) copy-start(f32[4,16,48]{0,1,2:T(8,128)} %copy.253) | copy-start | bytes 36868
  140.1 4.0 copy-start.13
  142.7 461.2 %all-reduce.2.cloned.1.call-start = ((), (), s32[]{:S(2)}) async-start(), calls=%async_computation.1 | async-start | bytes 786432 | tf_op jit(solution)/shard_map/psum | solution.py:243
  218.5 2.5 copy-start.19
  218.5 3.3 copy-start.9
  318.8 0.8 copy-start.7
  408.3 49.2 %copy-start.4 = (bf16[96,2048]{1,0:T(8,128)(2,1)S(1)}, bf16[96,2048]{1,0:T(8,128)(2,1)}, u32[]{:S(2)}) copy-start(bf16[96,2048]{1,0:T(8,128)(2,1)} %param.21) | copy-start | bytes 1179652
  408.4 49.2 %copy-start.10 = (f32[1,2048]{1,0:T(1,128)S(1)}, f32[1,2048]{1,0:T(1,128)}, u32[]{:S(2)}) copy-start(f32[1,2048]{1,0:T(1,128)} %get-tuple-element.308) | copy-start | bytes 24580
  457.8 1.2 copy-start.6
  459.0 2.4 copy-start.12
  459.0 2.4 copy-start.16
  459.0 2.4 copy-start.18
  459.0 145.8 %copy-start.11 = (f32[1,2048]{1,0:T(1,128)S(1)}, f32[1,2048]{1,0:T(1,128)}, u32[]{:S(2)}) copy-start(f32[1,2048]{1,0:T(1,128)} %get-tuple-element.311) | copy-start | bytes 24580
Sparse Core Ops, SparseCore 0:
  11.2 80.0 all-gather.6
  142.8 183.7 all-gather.8
  460.3 143.5 all-reduce.1
where the time goes:
time: 617 us; the launch traced here: 613 us
  blocking collectives  214 us (35%)
  waiting for transfers between devices  213 us (35%)
  other arithmetic  101 us (16%)
  local copies, waits for them, and re-layouts  40.3 us (7%)
  matrix products  29.8 us (5%)
  between operations  14.1 us (2%)
    psum x1, waiting for transfers between devices, per_device(): lax.psum(jnp.dot(hidden, down_weight, preferred_element_type=jnp.float32)...  142 us
    all_gather x2, blocking collectives, combined_all(): gathered = jax.tree.map(lambda a: lax.all_gather(a, axis), part)  97 us
    all_gather x1, blocking collectives, per_device(): collected = lax.all_gather(drafted[None], ('req', 'mp'), axis=0, tiled=True)  69.4 us
    all_gather x1, waiting for transfers between devices, per_device(): projected = lax.all_gather(own_projection, 'mp', axis=2, tiled=True)  64.1 us
    add x32, other arithmetic, fold_states(): mixed_left * factor_left[..., None] + mixed_right * factor_right[..., None]  54 us
    all_gather x1, blocking collectives, per_device(): projected_out = lax.all_gather(out_columns, 'mp', axis=1, tiled=True)  47.5 us
    add x32, other arithmetic, fold_states(): total_left * factor_left + total_right * factor_right  24.4 us
    unnamed x45, local copies, waits for them, and re-layouts  13.6 us
  transfers between devices with their start and end apart: 3, of which 3 were waited for; matrix products, arithmetic and copies ran while one was open for 5% of the time, Pallas kernels for 0%

commit v1 on v0

--- a/solution.py
+++ b/solution.py
@@ -240,8 +240,12 @@
     hidden = (jax.nn.silu(gate_up[:, 0]) * gate_up[:, 1]).astype(jnp.bfloat16)
     row_share = row_count // mp_count
     first_row = mp_place * row_share
-    summed = lax.psum(
-        jnp.dot(hidden, down_weight, preferred_element_type=jnp.float32).astype(jnp.bfloat16), "mp"
+    summed = jnp.sum(
+        lax.all_gather(
+            jnp.dot(hidden, down_weight, preferred_element_type=jnp.float32).astype(jnp.bfloat16),
+            "mp",
+        ),
+        axis=0,
     ).astype(jnp.float32)
     own_rows = lax.dynamic_slice_in_dim(summed, first_row, row_share, 0)
     residual_rows = lax.dynamic_slice_in_dim(residual, first_row, row_share, 0).astype(jnp.float32)

time: 617 us -> 597 us (0.968)
  waiting for transfers between devices: 213 us -> 188 us
  other arithmetic: 101 us -> 108 us
    psum x1 -> x0, waiting for transfers between devices: 142 us -> none  [per_device(): lax.psum(jnp.dot(hidden, down_weight, preferred_element_type=jnp.float32)...]
    all_gather x1, waiting for transfers between devices: 6.87 us -> 84.5 us  [combined_all(): gathered = jax.tree.map(lambda a: lax.all_gather(a, axis), part)]
    all_gather x0 -> x1, waiting for transfers between devices: none -> 39.2 us  [per_device(): lax.all_gather(jnp.dot(hidden, down_weight, preferred_element_type=jnp.fl...]
    reduce_sum x0 -> x1, other arithmetic: none -> 7.86 us  [per_device(): jnp.sum(lax.all_gather(jnp.dot(hidden, down_weight, preferred_element_typ...]
    unnamed x45 -> x47, local copies, waits for them, and re-layouts: 13.6 us -> 14.2 us
where the time goes in v1:
time: 597 us; the launch traced here: 592 us
  blocking collectives  213 us (36%)
  waiting for transfers between devices  188 us (31%)
  other arithmetic  108 us (18%)
  local copies, waits for them, and re-layouts  40.4 us (7%)
  matrix products  28 us (5%)
  between operations  14.1 us (2%)
    all_gather x2, blocking collectives, combined_all(): gathered = jax.tree.map(lambda a: lax.all_gather(a, axis), part)  96.7 us
    all_gather x1, waiting for transfers between devices, combined_all(): gathered = jax.tree.map(lambda a: lax.all_gather(a, axis), part)  84.5 us
    all_gather x1, blocking collectives, per_device(): collected = lax.all_gather(drafted[None], ('req', 'mp'), axis=0, tiled=True)  69.3 us
    all_gather x1, waiting for transfers between devices, per_device(): projected = lax.all_gather(own_projection, 'mp', axis=2, tiled=True)  64.1 us
    add x32, other arithmetic, fold_states(): mixed_left * factor_left[..., None] + mixed_right * factor_right[..., None]  54.1 us
    all_gather x1, blocking collectives, per_device(): projected_out = lax.all_gather(out_columns, 'mp', axis=1, tiled=True)  47.5 us
    all_gather x1, waiting for transfers between devices, per_device(): lax.all_gather(jnp.dot(hidden, down_weight, preferred_element_type=jnp.fl...  39.2 us
    add x32, other arithmetic, fold_states(): total_left * factor_left + total_right * factor_right  23.7 us
  transfers between devices with their start and end apart: 3, of which 3 were waited for; matrix products, arithmetic and copies ran while one was open for 5% of the time, Pallas kernels for 0%

profile of v1, /device:TPU:8, one launch (start us, length us, event | category | flops | bytes accessed | tf_op | source)
XLA Modules:
  0.0 592.3 jit_solution(13154351890688576730)
XLA Ops:
  7.2 1.7 fusion.81
  13.2 4.8 fusion.77
  18.1 3.9 copy.279
  22.0 4.0 copy.278
  27.2 64.1 %all-gather.9.cloned.1.call-done = bf16[96,3,2048]{0,2,1:T(8,128)(2,1)} async-done(((bf16[96,3,64]{0,2,1:T(8,128)(2,1)}), bf16[96,3,2048]{0,2,1:T(8,128)(2,1)}) %all-gather.9.cloned.1.call-update) | async-done | bytes 1179664 | tf_op jit(solution)/shard_map/all_gather | solution.py:181
  91.3 2.3 slice_convert_fusion.1
  93.6 2.5 copy.240
  96.1 1.3 copy.248
  97.4 1.6 multiply_reduce_fusion.1
  99.0 1.3 multiply_multiply_fusion.1
  100.5 1.3 multiply_subtract_fusion
  103.2 3.5 fusion.80
  107.0 2.4 fusion.20
  109.4 4.4 convolution_bitcast_fusion.1
  115.9 8.8 %fusion.17 = f32[48,16,128,2]{2,3,1,0:T(2,128)} fusion(f32[4,48,16,128]{3,1,2,0:T(8,128)} %convolution_bitcast_fusion.1, pred[4,2]{0,1:T(4,128)(4,1)S(1)} %get-tuple-element.271, f32[2,16,48]{0,1,2:T(8,128)S(1)} %select_reduce_fusion, f32[4,16,48]{0,1,2:T(8,128)S(1)} %copy.246), kind=kOutput, calls=%fused_computation.29 | convolution fusion | flops 9455616 | bytes 2377736 | tf_op jit(solution)/shard_map/prht,pthe->rthe/dot_general | solution.py:130
  124.7 2.8 multiply_reduce_fusion.2
  128.7 2.1 pad_maximum_fusion
  130.8 7.8 %conditional.1 = (f32[2,48,16]{1,2,0:T(8,128)}, f32[2,48,16]{1,2,0:T(8,128)S(1)}, f32[2,48,16,128]{3,2,1,0:T(8,128)S(1)}) conditional(s32[]{:T(128)} %convert_element_type.126, () %tuple.38, (f32[2,48,48]{1,2,0:T(8,128)S(1)}, bf16[96,16,128]{2,1,0:T(8,128)(2,1)}, bf16[2,48,16,128]{3,2,1,0:T(8,128)(2,1)S(1)}, bf16[96,3,2048]{0,2,1:T(8,128)(2,1)}) %tuple.104), branch_computations={%region_9.10_spmd, %region_10.13_spmd} | conditional | flops 38413824 | bytes 8417304 | solution.py:219
  130.8 2.5 copy.250
  134.4 2.0 fusion.76
  139.5 2.5 fusion.26
  142.1 46.7 %all-gather.2 = f32[64,48,16]{1,2,0:T(8,128)S(1)} all-gather(f32[2,48,16]{1,2,0:T(8,128)S(1)} %get-tuple-element.292), channel_id=4, replica_groups=mesh['req'=8,'mp'=32] {'mp'}, dimensions={0}, use_global_device_ids=true | all-gather | bytes 202752 | tf_op jit(solution)/shard_map/all_gather | solution.py:14
  188.8 50.0 %all-gather.1 = f32[64,48,16]{1,2,0:T(8,128)S(1)} all-gather(f32[2,48,16]{1,2,0:T(8,128)S(1)} %get-tuple-element.307), channel_id=3, replica_groups=mesh['req'=8,'mp'=32] {'mp'}, dimensions={0}, use_global_device_ids=true | all-gather | bytes 202752 | tf_op jit(solution)/shard_map/all_gather | solution.py:14
  239.6 84.5 %all-gather.11.cloned.1.call-done = f32[64,48,16,128]{3,2,1,0:T(8,128)} async-done(((f32[2,48,16,128]{3,2,1,0:T(8,128)}), f32[64,48,16,128]{3,2,1,0:T(8,128)}) %all-gather.11.cloned.1.call-update) | async-done | bytes 25165840 | tf_op jit(solution)/shard_map/all_gather | solution.py:14
  325.4 80.2 %while.19 = (s32[]{:T(128)}, f32[2,48,16]{1,2,0:T(8,128)S(1)}, f32[2,48,16]{1,2,0:T(8,128)S(1)}, f32[2,48,16,128]{3,2,1,0:T(8,128)S(1)}, f32[32,2,48,16]{2,3,1,0...) while((s32[]{:T(128)}, f32[2,48,16]{1,2,0:T(8,128)S(1)}, ...), condition=%wide.region_16.17_spmd, body=%wide.region_15.16_spmd.sunk | while | flops 599045 | bytes 2445455 | solution.py:19
  326.3 1.7 fusion.96
  328.9 1.7 fusion.96
  331.4 1.7 fusion.96
  334.0 1.7 fusion.96
  336.6 1.7 fusion.96
  339.2 1.7 fusion.96
  341.8 1.7 fusion.96
  344.4 1.7 fusion.96
  347.0 1.7 fusion.96
  349.6 1.7 fusion.96
  352.1 1.7 fusion.96
  354.7 1.7 fusion.96
  357.3 1.7 fusion.96
  359.9 1.7 fusion.96
  362.5 1.7 fusion.96
  365.1 1.7 fusion.96
  367.7 1.7 fusion.96
  370.2 1.7 fusion.96
  372.8 1.7 fusion.96
  375.4 1.7 fusion.96
  378.0 1.7 fusion.96
  380.6 1.7 fusion.96
  383.2 1.7 fusion.96
  385.8 1.7 fusion.96
  388.3 1.7 fusion.96
  390.9 1.7 fusion.96
  393.5 1.7 fusion.96
  396.1 1.7 fusion.96
  398.7 1.7 fusion.96
  401.3 1.7 fusion.96
  403.9 1.7 fusion.96
  405.9 1.3 convolution_convert_fusion.1
  407.2 47.5 %all_gather.41 = bf16[96,2048]{0,1:T(8,128)(2,1)S(1)} all-gather(bf16[96,64]{0,1:T(8,128)(2,1)S(1)} %convolution_convert_fusion.1), channel_id=1, replica_groups=mesh['req'=8,'mp'=32] {'mp'}, dimensions={1}, use_global_device_ids=true | all-gather | bytes 405504 | tf_op jit(solution)/shard_map/all_gather | solution.py:232
  459.8 69.3 %all-gather = bf16[512,4,64]{2,1,0:T(4,128)(2,1)S(1)} all-gather(bf16[2,4,64]{2,1,0:T(4,128)(2,1)S(1)} %add_convert_fusion.1), channel_id=2, replica_groups=mesh['req'=8,'mp'=32] {'req','mp'}, dimensions={0}, use_global_device_ids=true | all-gather | bytes 263168 | tf_op jit(solution)/shard_map/all_gather | solution.py:170
  529.5 2.7 copy.239
  532.2 1.9 convolution_bitcast_fusion.2
  537.0 39.2 %all-gather.13.cloned.1.call-done = bf16[3072,2048]{1,0:T(8,128)(2,1)} async-done(((bf16[96,2048]{1,0:T(8,128)(2,1)}), bf16[3072,2048]{1,0:T(8,128)(2,1)}) %all-gather.13.cloned.1.call-update) | async-done | bytes 12582928 | tf_op jit(solution)/shard_map/all_gather | solution.py:244
  576.2 7.9 %reduce_sum.113 = bf16[96,2048]{1,0:T(8,128)(2,1)S(1)} reduce(bf16[32,96,2048]{2,1,0:T(8,128)(2,1)} %bitcast.130, bf16[]{:T(256)} %constant.157.clone.1), dimensions={0}, to_apply=%region_18.19 | reduce | flops 6094848 | bytes 12976130 | tf_op jit(solution)/shard_map/reduce_sum | solution.py:243
  584.2 1.5 fusion.47
  (206 shorter events, 53.7 us)
Async XLA Ops:
  7.2 448.9 %copy-start = (bf16[2048,2,256]{2,1,0:T(2,128)(2,1)S(1)}, bf16[2048,2,256]{2,1,0:T(2,128)(2,1)}, u32[]{:S(2)}) copy-start(bf16[2048,2,256]{2,1,0:T(2,128)(2,1)} %param.30) | copy-start | bytes 6291460
  7.2 5.2 copy-start.1
  7.2 5.0 copy-start.16
  7.2 84.1 %all-gather.9.cloned.1.call-start = ((), (), s32[]{:S(2)}) async-start(), calls=%async_computation | async-start | bytes 1622016 | tf_op jit(solution)/shard_map/all_gather | solution.py:181
  9.7 314.5 %all-gather.11.cloned.1.call-start = ((), (), s32[]{:S(2)}) async-start(), calls=%async_computation.1 | async-start | bytes 25952256 | tf_op jit(solution)/shard_map/all_gather | solution.py:14
  12.4 5.7 copy-start.17
  12.4 118.4 %copy-start.9 = (f32[2,48,48]{1,2,0:T(8,128)}, f32[2,48,48]{1,2,0:T(8,128)S(1)}, u32[]{:S(2)}) copy-start(f32[2,48,48]{1,2,0:T(8,128)S(1)} %get-tuple-element.315) | copy-start | bytes 55300
  22.0 4.0 copy-start.19
  22.0 4.6 copy-start.12
  97.4 2.9 copy-start.3
  107.0 2.4 copy-start.2
  115.9 8.8 %copy-start.5 = (f32[4,16,48]{0,1,2:T(8,128)S(1)}, f32[4,16,48]{0,1,2:T(8,128)}, u32[]{:S(2)}) copy-start(f32[4,16,48]{0,1,2:T(8,128)} %copy.251) | copy-start | bytes 36868
  142.1 434.1 %all-gather.13.cloned.1.call-start = ((), (), s32[]{:S(2)}) async-start(), calls=%async_computation.2 | async-start | bytes 12976128 | tf_op jit(solution)/shard_map/all_gather | solution.py:244
  238.8 0.8 copy-start.8
  405.9 49.2 %copy-start.4 = (bf16[96,2048]{1,0:T(8,128)(2,1)S(1)}, bf16[96,2048]{1,0:T(8,128)(2,1)}, u32[]{:S(2)}) copy-start(bf16[96,2048]{1,0:T(8,128)(2,1)} %param.21) | copy-start | bytes 1179652
  405.9 49.2 %copy-start.13 = (f32[1,2048]{1,0:T(1,128)S(1)}, f32[1,2048]{1,0:T(1,128)}, u32[]{:S(2)}) copy-start(f32[1,2048]{1,0:T(1,128)} %get-tuple-element.308) | copy-start | bytes 24580
  455.3 0.7 copy-start.11
  456.0 1.2 copy-start.6
  457.3 1.9 copy-start.15
  457.3 2.0 copy-start.7
  532.2 2.6 copy-start.20
  532.2 2.6 copy-start.10
  532.2 4.0 copy-start.18
  576.2 8.0 %copy-start.14 = (f32[1,2048]{1,0:T(1,128)S(1)}, f32[1,2048]{1,0:T(1,128)}, u32[]{:S(2)}) copy-start(f32[1,2048]{1,0:T(1,128)} %get-tuple-element.311) | copy-start | bytes 24580
Sparse Core Ops, SparseCore 0:
  11.2 80.0 all-gather.8
  142.2 181.9 all-gather.10
  458.5 117.6 all-gather.12
